TPU v7x, 32 devices: a whole 2x2x4 slice. The times are simulated.
32 devices in a mesh: seq: 8 (over y, x, core), tp: 4 (over z).
Axes of the slice: x: 2, y: 2, z: 4, core: 2. Of those that a mesh axis runs over, the one named last changes fastest.
Arguments:
- hidden_states: bfloat16 [12288, 8192], P('seq', 'tp'), may hold values from -72 to 72
- positions: int32 [12288], P(('seq', 'tp')), may hold values from 0 to 32767
- key_weight: bfloat16 [8192, 1024], P('tp'), may hold values from -0.0625 to 0.0625
- value_weight: bfloat16 [8192, 1024], P('tp'), may hold values from -0.0625 to 0.0625
Outputs:
- keys: bfloat16 [12288, 1024], P(('seq', 'tp'))
- values: bfloat16 [12288, 1024], P(('seq', 'tp'))
- codes: bfloat16 [12288, 1024], P(('seq', 'tp'))
- page_bounds: float32 [1024, 2, 96], P(('seq', 'tp'))
All inputs are finite; a program needn't handle non-finite values.
Results may differ from a plain program's by a relative error of at most 0.008.
Values may be sent and summed in bfloat16 or wider, within the bound.
A program may use at most 128 MiB of HBM per device.

v0:
```python
import jax
import jax.numpy as jnp
from jax import lax
from jax.sharding import PartitionSpec as P

HEAD = 128
PAGE = 128


def rotate_keys(field, positions):
    count = field.shape[0]
    heads = field.reshape(count, -1, HEAD)
    half_width = HEAD // 2
    index = jnp.arange(half_width).astype(jnp.float32)
    frequency = jnp.exp(-jnp.log(jnp.float32(500000.0)) * 2.0 * index / HEAD)
    angles = positions.astype(jnp.float32)[:, None] * frequency[None, :]
    cosine = jnp.cos(angles)[:, None, :]
    sine = jnp.sin(angles)[:, None, :]
    front_half = heads[..., :half_width]
    back_half = heads[..., half_width:]
    turned = jnp.concatenate(
        [front_half * cosine - back_half * sine, back_half * cosine + front_half * sine], axis=-1
    )
    return turned.reshape(count, -1)


def smooth_codes(raw_keys, scale):
    ratio = raw_keys / scale
    return (ratio - jnp.sin(2.0 * jnp.pi * ratio) / (2.0 * jnp.pi)).astype(jnp.bfloat16)


def per_device(hidden_states, positions, key_weight, value_weight):
    width = key_weight.shape[1]
    summed = lax.psum_scatter(
        jnp.concatenate(
            [
                jnp.dot(hidden_states, key_weight, preferred_element_type=jnp.float32),
                jnp.dot(hidden_states, value_weight, preferred_element_type=jnp.float32),
            ],
            axis=1,
        ),
        "tp",
        scatter_dimension=0,
        tiled=True,
    )
    raw_keys = summed[:, :width]
    values = summed[:, width:].astype(jnp.bfloat16)
    peak = lax.pmax(jnp.max(jnp.abs(raw_keys), axis=0), ("seq", "tp"))
    scale = (peak + 1e-06) / 7.0
    codes = smooth_codes(raw_keys, scale)
    dequant = codes.astype(jnp.float32) * scale
    rotated = rotate_keys(dequant, positions)
    keys = rotated.astype(jnp.bfloat16)
    paged = rotated.reshape(-1, PAGE, width)
    page_low = jnp.min(paged, axis=1)
    page_high = jnp.max(paged, axis=1)
    local_bounds = jnp.transpose(jnp.stack([page_low, page_high], axis=0), (2, 0, 1))
    page_bounds = lax.all_to_all(
        local_bounds, ("seq", "tp"), split_axis=0, concat_axis=2, tiled=True
    )
    return (keys, values, codes, page_bounds)


def solution(mesh):
    return jax.shard_map(
        per_device,
        mesh=mesh,
        in_specs=(P("seq", "tp"), P(("seq", "tp")), P("tp", None), P("tp", None)),
        out_specs=(
            P(("seq", "tp"), None),
            P(("seq", "tp"), None),
            P(("seq", "tp"), None),
            P(("seq", "tp"), None, None),
        ),
        check_vma=False,
    )
```

profile of v0, /device:TPU:16, one launch (start us, length us, event | category | flops | bytes accessed | tf_op | source)
XLA Modules:
  0.0 331.2 jit_solution(4572473998549373964)
XLA Ops:
  7.2 0.0 reduce-scatter.2.cloned.1.call-start
  7.2 0.0 copy-start.3
  7.2 0.0 copy-start.4
  7.2 12.0 %fusion.3 = f32[1536,1024]{0,1:T(8,128)} fusion(bf16[1536,2048]{1,0:T(8,128)(2,1)} %param.4, bf16[2048,1024]{1,0:T(8,128)(2,1)} %param.6), kind=kOutput, calls=%fused_computation.17 | convolution fusion | flops 6442450944 | bytes 16777216 | tf_op jit(solution)/shard_map/dot_general | solution.py:37
  19.3 0.0 copy-done.3
  19.3 0.0 copy-done.4
  19.3 8.7 %fusion.4 = f32[1536,1024]{0,1:T(8,128)} fusion(bf16[1536,2048]{1,0:T(8,128)(2,1)S(1)} %copy-done.3, bf16[2048,1024]{1,0:T(8,128)(2,1)S(1)} %copy-done.4), kind=kOutput, calls=%fused_computation.18 | convolution fusion | flops 6442450944 | bytes 16777216 | tf_op jit(solution)/shard_map/dot_general | solution.py:38
  27.9 10.4 %pad_maximum_fusion = f32[1536,2048]{0,1:T(8,128)} fusion(f32[1536,1024]{0,1:T(8,128)} %fusion.4, f32[1536,1024]{0,1:T(8,128)} %fusion.3), kind=kLoop, calls=%fused_computation | loop fusion | flops 3145728 | bytes 25165824 | tf_op jit(solution)/shard_map/concatenate | solution.py:35
  38.4 0.0 copy-start.2
  38.4 0.0 reduce-scatter.2.cloned.1.call-update
  38.4 0.7 copy-done.2
  39.1 0.8 multiply_cosine_fusion
  39.8 212.7 %reduce-scatter.2.cloned.1.call-done = f32[384,2048]{0,1:T(8,128)} async-done(((f32[1536,2048]{0,1:T(8,128)}), f32[384,2048]{0,1:T(8,128)}) %reduce-scatter.2.cloned.1.call-update) | async-done | bytes 3145744 | tf_op jit(solution)/shard_map/reduce_scatter | solution.py:34
  252.5 1.6 abs_reduce_fusion
  254.1 39.3 %pmax.7 = f32[1024]{0:T(1024)S(1)} all-reduce(f32[1024]{0:T(1024)S(1)} %abs_reduce_fusion), channel_id=1, replica_groups=mesh['seq'=8,'tp'=4] {'seq','tp'}, use_global_device_ids=true, to_apply=%region_2.0 | all-reduce | flops 1024 | bytes 8192 | tf_op jit(solution)/shard_map/pmax | solution.py:48
  293.4 7.5 %convert_multiply_fusion = (f32[384,1024]{0,1:T(8,128)S(1)}, bf16[384,1024]{0,1:T(8,128)(2,1)}) fusion(f32[1024]{0:T(1024)S(1)} %add_multiply_fusion, f32[384,2048]{0,1:T(8,128)} %reduce-scatter.2.cloned.1.call-done), kind=kLoop, calls=%fused_computation.5 | loop fusion | flops 2752512 | bytes 3936256 | tf_op jit(solution)/shard_map/mul | solution.py:51
  300.9 1.0 fusion.2
  301.9 0.6 copy.41
  302.5 1.7 copy.42
  304.2 0.3 multiply_subtract_fusion
  304.6 1.4 fusion.1
  305.9 0.2 reshape_reshape.3
  306.2 0.2 fusion
  306.3 0.0 copy-start.1
  306.4 0.6 copy.34
  307.0 0.0 copy-start
  307.0 2.3 reshape.66
  309.2 5.8 %all-to-all-start = ((f32[32,1,192]{2,1,0:T(1,128)}), f32[32,1,192]{2,1,0:T(1,128)S(1)}, u32[]{:S(2)}, u32[]{:S(2)}) async-start(f32[32,1,192]{2,1,0:T(1,128)} %reshape.66), calls=%async_computation.1 | async-start | bytes 65536 | tf_op jit(solution)/shard_map/all_to_all | solution.py:58
  315.0 0.0 copy-done.1
  315.0 1.1 copy.45
  316.1 0.0 copy-done
  316.1 1.2 copy.38
  317.3 1.5 slice.24
  318.8 1.2 copy.37
  319.9 0.2 all-to-all-done
  320.1 0.5 broadcast.49
  320.7 0.7 reduce
  321.4 1.5 reshape.67
  322.9 0.6 copy.40
  323.6 0.1 copy.36
  323.7 0.7 copy.39
  (4 shorter events, 0.0 us)
Async XLA Ops:
  7.2 245.4 %reduce-scatter.2.cloned.1.call-start = ((), (), s32[]{:S(2)}) async-start(), calls=%async_computation.2 | async-start | bytes 15728640 | tf_op jit(solution)/shard_map/reduce_scatter | solution.py:34
  7.2 12.1 %copy-start.3 = (bf16[1536,2048]{1,0:T(8,128)(2,1)S(1)}, bf16[1536,2048]{1,0:T(8,128)(2,1)}, u32[]{:S(2)}) copy-start(bf16[1536,2048]{1,0:T(8,128)(2,1)} %param.4) | copy-start | bytes 18874372
  7.2 12.0 %copy-start.4 = (bf16[2048,1024]{1,0:T(8,128)(2,1)S(1)}, bf16[2048,1024]{1,0:T(8,128)(2,1)}, u32[]{:S(2)}) copy-start(bf16[2048,1024]{1,0:T(8,128)(2,1)} %param.7) | copy-start | bytes 12582916
  38.4 0.7 copy-start.2
  306.3 8.7 %copy-start.1 = (bf16[384,8,128]{2,1,0:T(8,128)(2,1)S(1)}, bf16[384,8,128]{2,1,0:T(8,128)(2,1)}, u32[]{:S(2)}) copy-start(bf16[384,8,128]{2,1,0:T(8,128)(2,1)} %get-tuple-element.26) | copy-start | bytes 2359300
  307.0 9.1 %copy-start = (bf16[384,1024]{0,1:T(8,128)(2,1)S(1)}, bf16[384,1024]{0,1:T(8,128)(2,1)}, u32[]{:S(2)}) copy-start(bf16[384,1024]{0,1:T(8,128)(2,1)} %get-tuple-element.29) | copy-start | bytes 2359300
  309.2 10.9 %all-to-all-start = ((f32[32,1,192]{2,1,0:T(1,128)}), f32[32,1,192]{2,1,0:T(1,128)S(1)}, u32[]{:S(2)}, u32[]{:S(2)}) async-start(f32[32,1,192]{2,1,0:T(1,128)} %reshape.66), calls=%async_computation.1 | async-start | bytes 65536 | tf_op jit(solution)/shard_map/all_to_all | solution.py:58
Sparse Core Ops, SparseCore 0:
  38.5 213.9 reduce-scatter.1
where the time goes:
time: 335 us; the launch traced here: 331 us
  waiting for transfers between devices  213 us (64%)
  blocking collectives  39.3 us (12%)
  other arithmetic  22.9 us (7%)
  matrix products  20.7 us (6%)
  local copies, waits for them, and re-layouts  15.4 us (5%)
  between operations  14.2 us (4%)
  starting transfers between devices  5.83 us (2%)
    reduce_scatter x1, waiting for transfers between devices, per_device(): lax.psum_scatter(jnp.concatenate([jnp.dot(hidden_states, key_weight, pref...  213 us
    pmax x1, blocking collectives, per_device(): peak = lax.pmax(jnp.max(jnp.abs(raw_keys), axis=0), ('seq', 'tp'))  39.3 us
    dot_general x1, matrix products, per_device(): jnp.dot(hidden_states, key_weight, preferred_element_type=jnp.float32)  12 us
    unnamed x18, local copies, waits for them, and re-layouts  10.8 us
    concatenate x1, other arithmetic, per_device(): jnp.concatenate([jnp.dot(hidden_states, key_weight, preferred_element_typ...  10.4 us
    dot_general x1, matrix products, per_device(): jnp.dot(hidden_states, value_weight, preferred_element_type=jnp.float32)  8.67 us
    mul x1, other arithmetic, per_device(): dequant = codes.astype(jnp.float32) * scale  7.5 us
  transfers between devices with their start and end apart: 2, of which 2 were waited for; matrix products, arithmetic and copies ran while one was open for 2% of the time, Pallas kernels for 0%

commit v1 on v0

v1 whole, which is shorter than its diff:
```python
import functools
import math

import jax
import jax.numpy as jnp
from jax import lax
from jax.experimental import pallas as pl
from jax.experimental.pallas import tpu as pltpu
from jax.sharding import PartitionSpec as P

HEAD = 128
PAGE = 128
CW = 256
DEPTH = 4
MESH = pl.DeviceIdType.MESH


def sine_of_turns(turns):
    rest = turns - jnp.round(turns)
    size = jnp.abs(rest)
    x = (2.0 * math.pi) * jnp.minimum(size, 0.5 - size)
    y = x * x
    poly = jnp.float32(-1.0 / math.factorial(11))
    for order, sign in ((9, 1.0), (7, -1.0), (5, 1.0), (3, -1.0), (1, 1.0)):
        poly = poly * y + jnp.float32(sign / math.factorial(order))
    wave = poly * x
    return jnp.where(rest < 0.0, -wave, wave)


def kernel(
    n_seq, n_tp,
    hidden, pos, key_w, value_w,
    keys_out, values_out, codes_out, bounds_out,
    hb, wb, sb, rr, rl, acc, raw, cos_s, sin_s,
    keys_s, codes_s, values_s,
    peak_own, peak_tp, peak_mid, peak_seq,
    bnd_own, bnd_seq, bnd_tp, bnd_pages, bnd_turned, bnd_res,
    h_sem, w_sem, send_sem, rr_sem, rl_sem, out_sem,
    ptp_send, ptp_recv, psq_send, psq_recv, bsq_send, bsq_recv, btp_send, btp_recv,
):
    s = lax.axis_index("seq")
    t = lax.axis_index("tp")
    rows = hb.shape[1]
    width = raw.shape[1]
    nch = width // CW
    per_phase = (n_tp - 1) * nch
    steps = 2 * per_phase
    pages = rows // PAGE

    def load_h(b):
        return pltpu.make_async_copy(hidden.at[pl.ds(b * rows, rows), :], hb.at[b], h_sem.at[b])

    def load_w(ch):
        src = key_w if ch < nch else value_w
        return pltpu.make_async_copy(src.at[:, pl.ds((ch % nch) * CW, CW)], wb.at[ch], w_sem.at[ch])

    load_w(0).start()
    load_h(n_tp - 1).start()
    load_h(0).start()
    for ch in range(1, nch):
        load_w(ch).start()
    for b in range(1, n_tp - 1):
        load_h(b).start()
    for ch in range(nch, 2 * nch):
        load_w(ch).start()

    barrier = pltpu.get_barrier_semaphore()
    for d in range(1, n_tp):
        pl.semaphore_signal(barrier, inc=1, device_id={"tp": lax.rem(t + d, n_tp)}, device_id_type=MESH)
    for d in range(1, n_seq):
        pl.semaphore_signal(barrier, inc=1, device_id={"seq": lax.rem(s + d, n_seq)}, device_id_type=MESH)
    pl.semaphore_wait(barrier, n_tp - 1 + n_seq - 1)

    def send_right(b, ch):
        return pltpu.make_async_remote_copy(
            sb.at[b, ch], rr.at[b, ch], send_sem.at[b, ch], rr_sem.at[b, ch],
            device_id={"tp": jnp.minimum(t + 1, n_tp - 1)}, device_id_type=MESH)

    def send_left(b, ch):
        return pltpu.make_async_remote_copy(
            sb.at[b, ch], rl.at[b, ch], send_sem.at[b, ch], rl_sem.at[b, ch],
            device_id={"tp": jnp.maximum(t - 1, 0)}, device_id_type=MESH)

    def place(i):
        q = lax.rem(i, per_phase)
        turn = q // nch
        c = lax.rem(q, nch)
        return turn, c, (i // per_phase) * nch + c

    def wait_sends(i):
        turn, _, ch = place(i)

        @pl.when(n_tp - 1 - turn > t)
        def _():
            send_right(n_tp - 1 - turn, ch).wait_send()

        @pl.when(turn < t)
        def _():
            send_left(turn, ch).wait_send()

    def fill_angles():
        lane = lax.broadcasted_iota(jnp.int32, (1, HEAD), 1)
        half = HEAD // 2
        index = jnp.where(lane < half, lane, lane - half).astype(jnp.float32)
        frequency = jnp.exp(-jnp.log(jnp.float32(500000.0)) * 2.0 * index / HEAD)
        for j in range(pages):
            row = pos[j:j + 1, :].astype(jnp.float32)
            column = jnp.transpose(jnp.broadcast_to(row, (PAGE, PAGE)))
            angles = column * frequency
            sine = jnp.sin(angles)
            cos_s[j * PAGE:(j + 1) * PAGE, :] = jnp.cos(angles)
            sin_s[j * PAGE:(j + 1) * PAGE, :] = jnp.where(lane < half, -sine, sine)

    def own_sum(ch):
        acc[...] = jnp.dot(hb[t], wb[ch], preferred_element_type=jnp.float32)

        @pl.when(t > 0)
        def _():
            send_right(t, ch).wait_recv()
            acc[...] += rr[t, ch].astype(jnp.float32)

        @pl.when(t < n_tp - 1)
        def _():
            send_left(t, ch).wait_recv()
            acc[...] += rl[t, ch].astype(jnp.float32)

    def tp_copies(src, dst, send, recv, own):
        return [
            pltpu.make_async_remote_copy(
                src, dst.at[t if own else d], send.at[d], recv.at[d],
                device_id={"tp": lax.rem(t + d, n_tp)}, device_id_type=MESH)
            for d in range(1, n_tp)
        ]

    def peak_tp_copies():
        return tp_copies(peak_own, peak_tp, ptp_send, ptp_recv, False)

    def peak_seq_copies():
        return [
            pltpu.make_async_remote_copy(
                peak_mid, peak_seq.at[d], psq_send.at[d], psq_recv.at[d],
                device_id={"seq": lax.rem(s + d, n_seq)}, device_id_type=MESH)
            for d in range(1, n_seq)
        ]

    group = width // n_seq
    tile = bnd_seq.shape[2]

    def tile_of(other):
        return pl.ds(pl.multiple_of((other * group) // tile * tile, 128), tile)

    def bound_seq_copies():
        out = []
        for d in range(1, n_seq):
            other = lax.rem(s + d, n_seq)
            out.append(pltpu.make_async_remote_copy(
                bnd_own.at[:, tile_of(other)], bnd_seq.at[s], bsq_send.at[d], bsq_recv.at[d],
                device_id={"seq": other}, device_id_type=MESH))
        return out

    def bound_tp_copies():
        return tp_copies(bnd_seq, bnd_tp, btp_send, btp_recv, True)

    def key_sums():
        def one(c, carry):
            own_sum(c)
            total = acc[...]
            lanes = pl.ds(pl.multiple_of(c * CW, 128), CW)
            raw[:, lanes] = total
            peak_own[:, lanes] = jnp.max(jnp.abs(total).reshape(rows // 8, 8, CW), axis=0)
            return carry

        lax.fori_loop(0, nch, one, 0)
        for copy in peak_tp_copies():
            copy.start()

    def peak_middle():
        best = peak_own[...]
        for copy in peak_tp_copies():
            copy.wait_recv()
        for d in range(1, n_tp):
            best = jnp.maximum(best, peak_tp[d])
        peak_mid[...] = best
        for copy in peak_seq_copies():
            copy.start()

    def finish_keys():
        for copy in peak_seq_copies():
            copy.wait_recv()
        best = peak_mid[...]
        for d in range(1, n_seq):
            best = jnp.maximum(best, peak_seq[d])
        peak_tp[0] = best
        bnd_own[...] = jnp.zeros_like(bnd_own)

        def one(h, carry):
            lanes = pl.ds(pl.multiple_of(h * HEAD, 128), HEAD)
            peak = jnp.max(peak_tp[0, :, lanes], axis=0, keepdims=True)
            scale = (peak + 1e-06) / 7.0
            inverse = 1.0 / scale
            for j in range(pages):
                part = pl.ds(j * PAGE, PAGE)
                ratio = raw[part, lanes] * inverse
                code = (ratio - sine_of_turns(ratio) * (1.0 / (2.0 * math.pi))).astype(jnp.bfloat16)
                codes_s[part, lanes] = code
                dequant = code.astype(jnp.float32) * scale
                turned = dequant * cos_s[part, :] + pltpu.roll(dequant, HEAD // 2, 1) * sin_s[part, :]
                keys_s[part, lanes] = turned.astype(jnp.bfloat16)
                bnd_own[j:j + 1, lanes] = jnp.min(turned, axis=0, keepdims=True)
                bnd_own[pages + j:pages + j + 1, lanes] = jnp.max(turned, axis=0, keepdims=True)
            return carry

        lax.fori_loop(0, width // HEAD, one, 0)
        for copy in bound_seq_copies():
            copy.start()
        pltpu.make_async_copy(codes_s, codes_out, out_sem.at[0]).start()
        pltpu.make_async_copy(keys_s, keys_out, out_sem.at[1]).start()
        bnd_seq[s] = bnd_own[:, tile_of(s)]

    def bounds_middle():
        for copy in bound_seq_copies():
            copy.wait_recv()
        for copy in bound_tp_copies():
            copy.start()
        bnd_tp[t] = bnd_seq[...]

    def finish_bounds():
        for copy in bound_tp_copies():
            copy.wait_recv()
        channels = width // (n_seq * n_tp)
        inside = lax.rem(s * group, tile) + t * channels
        for side in range(2):
            bnd_pages[...] = jnp.zeros_like(bnd_pages)
            for a in range(n_seq):
                for b in range(n_tp):
                    first = (a * n_tp + b) * pages
                    bnd_pages[first:first + pages, :] = bnd_tp[b, a, side * pages:(side + 1) * pages, :]
            bnd_turned[...] = jnp.transpose(bnd_pages[...])
            mine = bnd_turned[pl.ds(pl.multiple_of(inside, 8), channels), :]
            bnd_res[side] = mine[:, :bnd_res.shape[2]]
        pltpu.make_async_copy(bnd_res, bounds_out, out_sem.at[2]).start()

    def body(i, carry):
        turn, c, ch = place(i)

        @pl.when(turn == 0)
        def _():
            pltpu.make_async_copy(key_w.at[:, pl.ds(0, CW)], wb.at[ch], w_sem.at[ch]).wait()

        for o in range(n_tp // 2):
            @pl.when(i == o * nch)
            def _(o=o):
                load_h(o).wait()
                load_h(n_tp - 1 - o).wait()

        @pl.when(i >= DEPTH)
        def _():
            wait_sends(i - DEPTH)

        right = n_tp - 1 - turn
        left = turn

        @pl.when(right > t)
        def _():
            acc[...] = jnp.dot(hb[right], wb[ch], preferred_element_type=jnp.float32)

            @pl.when(t > 0)
            def _():
                send_right(right, ch).wait_recv()
                acc[...] += rr[right, ch].astype(jnp.float32)

            sb[right, ch] = acc[...].astype(jnp.bfloat16)
            send_right(right, ch).start()

        @pl.when(left < t)
        def _():
            acc[...] = jnp.dot(hb[left], wb[ch], preferred_element_type=jnp.float32)

            @pl.when(t < n_tp - 1)
            def _():
                send_left(left, ch).wait_recv()
                acc[...] += rl[left, ch].astype(jnp.float32)

            sb[left, ch] = acc[...].astype(jnp.bfloat16)
            send_left(left, ch).start()

        for when, work in (
            (2, fill_angles),
            (per_phase, key_sums),
            (per_phase + 1, peak_middle),
            (per_phase + 3, finish_keys),
            (per_phase + 5, bounds_middle),
            (per_phase + 7, finish_bounds),
        ):
            pl.when(i == when)(work)
        return carry

    lax.fori_loop(0, steps, body, 0)

    def last(c, carry):
        own_sum(nch + c)
        values_s[c] = acc[...].astype(jnp.bfloat16)
        lanes = pl.ds(pl.multiple_of(c * CW, 128), CW)
        pltpu.make_async_copy(values_s.at[c], values_out.at[:, lanes], out_sem.at[3 + c]).start()
        return carry

    lax.fori_loop(0, nch, last, 0)

    def drain(i, carry):
        wait_sends(i)
        return carry

    lax.fori_loop(steps - DEPTH, steps, drain, 0)
    for copy in peak_tp_copies() + peak_seq_copies() + bound_seq_copies() + bound_tp_copies():
        copy.wait_send()
    pltpu.make_async_copy(codes_s, codes_out, out_sem.at[0]).wait()
    pltpu.make_async_copy(keys_s, keys_out, out_sem.at[1]).wait()
    pltpu.make_async_copy(bnd_res, bounds_out, out_sem.at[2]).wait()
    for c in range(nch):
        pltpu.make_async_copy(values_s.at[c], values_out.at[:, pl.ds(c * CW, CW)], out_sem.at[3 + c]).wait()


def per_device(n_seq, n_tp, hidden_states, positions, key_weight, value_weight):
    depth, width = key_weight.shape
    rows = hidden_states.shape[0] // n_tp
    nch = width // CW
    pages = rows // PAGE
    all_pages = pages * n_seq * n_tp
    padded_pages = -(-all_pages // 128) * 128
    tile = max(128, width // n_seq)
    channels = width // (n_seq * n_tp)
    bf16, f32 = jnp.bfloat16, jnp.float32
    dma = pltpu.SemaphoreType.DMA
    hbm = pl.BlockSpec(memory_space=pl.ANY)
    keys, values, codes, bounds = pl.pallas_call(
        functools.partial(kernel, n_seq, n_tp),
        out_shape=(
            jax.ShapeDtypeStruct((rows, width), bf16),
            jax.ShapeDtypeStruct((rows, width), bf16),
            jax.ShapeDtypeStruct((rows, width), bf16),
            jax.ShapeDtypeStruct((2, channels, all_pages), f32),
        ),
        in_specs=[hbm, pl.BlockSpec(memory_space=pltpu.VMEM), hbm, hbm],
        out_specs=(hbm, hbm, hbm, hbm),
        scratch_shapes=[
            pltpu.VMEM((n_tp, rows, depth), bf16),
            pltpu.VMEM((2 * nch, depth, CW), bf16),
            pltpu.VMEM((n_tp, 2 * nch, rows, CW), bf16),
            pltpu.VMEM((n_tp, 2 * nch, rows, CW), bf16),
            pltpu.VMEM((n_tp, 2 * nch, rows, CW), bf16),
            pltpu.VMEM((rows, CW), f32),
            pltpu.VMEM((rows, width), f32),
            pltpu.VMEM((rows, HEAD), f32),
            pltpu.VMEM((rows, HEAD), f32),
            pltpu.VMEM((rows, width), bf16),
            pltpu.VMEM((rows, width), bf16),
            pltpu.VMEM((nch, rows, CW), bf16),
            pltpu.VMEM((8, width), f32),
            pltpu.VMEM((n_tp, 8, width), f32),
            pltpu.VMEM((8, width), f32),
            pltpu.VMEM((n_seq, 8, width), f32),
            pltpu.VMEM((8, width), f32),
            pltpu.VMEM((n_seq, 8, tile), f32),
            pltpu.VMEM((n_tp, n_seq, 8, tile), f32),
            pltpu.VMEM((padded_pages, tile), f32),
            pltpu.VMEM((tile, padded_pages), f32),
            pltpu.VMEM((2, channels, all_pages), f32),
            dma((n_tp,)),
            dma((2 * nch,)),
            dma((n_tp, 2 * nch)),
            dma((n_tp, 2 * nch)),
            dma((n_tp, 2 * nch)),
            dma((3 + nch,)),
            dma((n_tp,)), dma((n_tp,)),
            dma((n_seq,)), dma((n_seq,)),
            dma((n_seq,)), dma((n_seq,)),
            dma((n_tp,)), dma((n_tp,)),
        ],
        compiler_params=pltpu.CompilerParams(
            collective_id=0, has_side_effects=True, vmem_limit_bytes=56 * 2**20
        ),
        cost_estimate=pl.CostEstimate(
            flops=2 * n_tp * rows * depth * 2 * width,
            bytes_accessed=2 * (n_tp * rows * depth + 2 * depth * width + 3 * rows * width),
            transcendentals=0,
        ),
    )(hidden_states, positions.reshape(pages, PAGE), key_weight, value_weight)
    return keys, values, codes, jnp.transpose(bounds, (1, 0, 2))


def solution(mesh):
    return jax.shard_map(
        functools.partial(per_device, mesh.shape["seq"], mesh.shape["tp"]),
        mesh=mesh,
        in_specs=(P("seq", "tp"), P(("seq", "tp")), P("tp", None), P("tp", None)),
        out_specs=(
            P(("seq", "tp"), None),
            P(("seq", "tp"), None),
            P(("seq", "tp"), None),
            P(("seq", "tp"), None, None),
        ),
        check_vma=False,
    )
```

time: 335 us -> 164 us (0.49); the launches traced: 331 us -> 164 us
  waiting for transfers between devices: 213 us -> 0 us
  Pallas kernels: 0 us -> 155 us
  blocking collectives: 39.3 us -> 0 us
  other arithmetic: 22.9 us -> 0 us
  matrix products: 20.7 us -> 0 us
  between operations: 14.2 us -> 0.64 us
  local copies, waits for them, and re-layouts: 15.4 us -> 7.59 us
  starting transfers between devices: 5.83 us -> 0 us
    reduce_scatter x1 -> x0, waiting for transfers between devices: 213 us -> none  [per_device(): lax.psum_scatter(jnp.concatenate([jnp.dot(hidden_states, key_weight, pref...]
    pallas_call x0 -> x1, Pallas kernels: none -> 155 us  [per_device(): pl.pallas_call(functools.partial(kernel, n_seq, n_tp), out_shape=(jax.Sha...]
    pmax x1 -> x0, blocking collectives: 39.3 us -> none  [per_device(): peak = lax.pmax(jnp.max(jnp.abs(raw_keys), axis=0), ('seq', 'tp'))]
    dot_general x2 -> x0, matrix products: 20.7 us -> none  [the longest x1 12 us: per_device(): jnp.dot(hidden_states, key_weight, preferred_element_type=jnp.float32)]
    concatenate x1 -> x0, other arithmetic: 10.4 us -> none  [per_device(): jnp.concatenate([jnp.dot(hidden_states, key_weight, preferred_element_typ...]
    mul x1 -> x0, other arithmetic: 7.5 us -> none  [per_device(): dequant = codes.astype(jnp.float32) * scale]
    all_to_all x1 -> x0, starting transfers between devices: 5.79 us -> none  [per_device(): lax.all_to_all(local_bounds, ('seq', 'tp'), split_axis=0, concat_axis=2,...]
    unnamed x18 -> x4, local copies, waits for them, and re-layouts: 10.8 us -> 7.59 us
  transfers between devices with their start and end apart: 2 -> 0, of which waited for: 2 -> 0; matrix products, arithmetic and copies ran while one was open for 2% -> 0% of each run, Pallas kernels for 0% -> 0%
where the time goes in v1:
time: 164 us
  Pallas kernels  155 us (95%)
  local copies, waits for them, and re-layouts  7.59 us (5%)
    pallas_call x1, Pallas kernels, per_device(): pl.pallas_call(functools.partial(kernel, n_seq, n_tp), out_shape=(jax.Sha...  155 us
    unnamed x4, local copies, waits for them, and re-layouts  7.59 us

profile of v1, /device:TPU:16, one launch (start us, length us, event | category | flops | bytes accessed | tf_op | source)
XLA Modules:
  0.0 163.6 jit_solution(1496141031913536069)
XLA Ops:
  0.6 155.4 %shard_map.75 = (bf16[384,1024]{1,0:T(8,128)(2,1)}, bf16[384,1024]{1,0:T(8,128)(2,1)}, bf16[384,1024]{1,0:T(8,128)(2,1)}, f32[2,32,96]{2,1,0:T(8,128)}) custom-call(bf16[1536,2048]{1,0:T(8,128)(2,1)} %hidden.1, s32[3,128]{1,0:T(4,128)} %bitcast.3, bf16[2048,1024]{1,0:T(8,128)(2,1)} %key_w.1, bf16[2048,1024]{1,0:T(8,128)(2,1)} %value_w.1), custom_call_target="tpu_custom_call" | custom-call | flops 12884901888 | bytes 17039360 | tf_op jit(solution)/shard_map/pallas_call | solution.py:335
  156.0 1.4 copy.8
  157.4 2.1 %copy.12 = bf16[384,1024]{1,0:T(8,128)(2,1)} copy(bf16[384,1024]{1,0:T(8,128)(2,1)} %get-tuple-element.20) | data formatting | bytes 1572864
  159.5 2.1 %copy.13 = bf16[384,1024]{1,0:T(8,128)(2,1)} copy(bf16[384,1024]{1,0:T(8,128)(2,1)} %get-tuple-element.21) | data formatting | bytes 1572864
  161.6 2.1 %copy.14 = bf16[384,1024]{1,0:T(8,128)(2,1)} copy(bf16[384,1024]{1,0:T(8,128)(2,1)} %get-tuple-element.22) | data formatting | bytes 1572864

commit v2 on v1

--- a/solution.py
+++ b/solution.py
@@ -11,7 +11,7 @@
 HEAD = 128
 PAGE = 128
 CW = 256
-DEPTH = 4
+DEPTH = 12
 MESH = pl.DeviceIdType.MESH
 
 
@@ -87,16 +87,24 @@
         c = lax.rem(q, nch)
         return turn, c, (i // per_phase) * nch + c
 
+    def right_job(j, run):
+        turn, _, ch = place(jnp.clip(j, 0, steps - 1))
+        b = n_tp - 1 - turn
+
+        @pl.when((j >= 0) & (j < steps) & (b > t))
+        def _():
+            run(b, ch)
+
+    def left_job(j, run):
+        turn, _, ch = place(jnp.clip(j, 0, steps - 1))
+
+        @pl.when((j >= 0) & (j < steps) & (turn < t))
+        def _():
+            run(turn, ch)
+
     def wait_sends(i):
-        turn, _, ch = place(i)
-
-        @pl.when(n_tp - 1 - turn > t)
-        def _():
-            send_right(n_tp - 1 - turn, ch).wait_send()
-
-        @pl.when(turn < t)
-        def _():
-            send_left(turn, ch).wait_send()
+        right_job(i - t, lambda b, ch: send_right(b, ch).wait_send())
+        left_job(i - (n_tp - 1 - t), lambda b, ch: send_left(b, ch).wait_send())
 
     def fill_angles():
         lane = lax.broadcasted_iota(jnp.int32, (1, HEAD), 1)
@@ -240,10 +248,32 @@
             bnd_res[side] = mine[:, :bnd_res.shape[2]]
         pltpu.make_async_copy(bnd_res, bounds_out, out_sem.at[2]).start()
 
+    def forward_right(b, ch):
+        acc[...] = jnp.dot(hb[b], wb[ch], preferred_element_type=jnp.float32)
+
+        @pl.when(t > 0)
+        def _():
+            send_right(b, ch).wait_recv()
+            acc[...] += rr[b, ch].astype(jnp.float32)
+
+        sb[b, ch] = acc[...].astype(jnp.bfloat16)
+        send_right(b, ch).start()
+
+    def forward_left(b, ch):
+        acc[...] = jnp.dot(hb[b], wb[ch], preferred_element_type=jnp.float32)
+
+        @pl.when(t < n_tp - 1)
+        def _():
+            send_left(b, ch).wait_recv()
+            acc[...] += rl[b, ch].astype(jnp.float32)
+
+        sb[b, ch] = acc[...].astype(jnp.bfloat16)
+        send_left(b, ch).start()
+
     def body(i, carry):
-        turn, c, ch = place(i)
-
-        @pl.when(turn == 0)
+        turn, c, ch = place(jnp.minimum(i, steps - 1))
+
+        @pl.when((turn == 0) & (i < steps))
         def _():
             pltpu.make_async_copy(key_w.at[:, pl.ds(0, CW)], wb.at[ch], w_sem.at[ch]).wait()
 
@@ -253,49 +283,22 @@
                 load_h(o).wait()
                 load_h(n_tp - 1 - o).wait()
 
-        @pl.when(i >= DEPTH)
-        def _():
-            wait_sends(i - DEPTH)
-
-        right = n_tp - 1 - turn
-        left = turn
-
-        @pl.when(right > t)
-        def _():
-            acc[...] = jnp.dot(hb[right], wb[ch], preferred_element_type=jnp.float32)
-
-            @pl.when(t > 0)
-            def _():
-                send_right(right, ch).wait_recv()
-                acc[...] += rr[right, ch].astype(jnp.float32)
-
-            sb[right, ch] = acc[...].astype(jnp.bfloat16)
-            send_right(right, ch).start()
-
-        @pl.when(left < t)
-        def _():
-            acc[...] = jnp.dot(hb[left], wb[ch], preferred_element_type=jnp.float32)
-
-            @pl.when(t < n_tp - 1)
-            def _():
-                send_left(left, ch).wait_recv()
-                acc[...] += rl[left, ch].astype(jnp.float32)
-
-            sb[left, ch] = acc[...].astype(jnp.bfloat16)
-            send_left(left, ch).start()
+        wait_sends(i - DEPTH)
+        right_job(i - t, forward_right)
+        left_job(i - (n_tp - 1 - t), forward_left)
 
         for when, work in (
             (2, fill_angles),
             (per_phase, key_sums),
-            (per_phase + 1, peak_middle),
-            (per_phase + 3, finish_keys),
-            (per_phase + 5, bounds_middle),
-            (per_phase + 7, finish_bounds),
+            (per_phase + 2, peak_middle),
+            (per_phase + 5, finish_keys),
+            (per_phase + 7, bounds_middle),
+            (per_phase + 9, finish_bounds),
         ):
             pl.when(i == when)(work)
         return carry
 
-    lax.fori_loop(0, steps, body, 0)
+    lax.fori_loop(0, steps + n_tp - 2, body, 0)
 
     def last(c, carry):
         own_sum(nch + c)
@@ -310,7 +313,7 @@
         wait_sends(i)
         return carry
 
-    lax.fori_loop(steps - DEPTH, steps, drain, 0)
+    lax.fori_loop(steps + n_tp - 2 - DEPTH, steps + n_tp - 2, drain, 0)
     for copy in peak_tp_copies() + peak_seq_copies() + bound_seq_copies() + bound_tp_copies():
         copy.wait_send()
     pltpu.make_async_copy(codes_s, codes_out, out_sem.at[0]).wait()

time: 164 us -> 123 us (0.75)
  Pallas kernels: 155 us -> 115 us
    pallas_call x1, Pallas kernels: 155 us -> 115 us  [per_device(): pl.pallas_call(functools.partial(kernel, n_seq, n_tp), out_shape=(jax.Sha...]
where the time goes in v2:
time: 123 us
  Pallas kernels  115 us (93%)
  local copies, waits for them, and re-layouts  7.59 us (6%)
    pallas_call x1, Pallas kernels, per_device(): pl.pallas_call(functools.partial(kernel, n_seq, n_tp), out_shape=(jax.Sha...  115 us
    unnamed x4, local copies, waits for them, and re-layouts  7.59 us

profile of v2, /device:TPU:16, one launch (start us, length us, event | category | flops | bytes accessed | tf_op | source)
XLA Modules:
  0.0 122.8 jit_solution(612269235337302003)
XLA Ops:
  0.6 114.6 %shard_map.75 = (bf16[384,1024]{1,0:T(8,128)(2,1)}, bf16[384,1024]{1,0:T(8,128)(2,1)}, bf16[384,1024]{1,0:T(8,128)(2,1)}, f32[2,32,96]{2,1,0:T(8,128)}) custom-call(bf16[1536,2048]{1,0:T(8,128)(2,1)} %hidden.1, s32[3,128]{1,0:T(4,128)} %bitcast.3, bf16[2048,1024]{1,0:T(8,128)(2,1)} %key_w.1, bf16[2048,1024]{1,0:T(8,128)(2,1)} %value_w.1), custom_call_target="tpu_custom_call" | custom-call | flops 12884901888 | bytes 17039360 | tf_op jit(solution)/shard_map/pallas_call | solution.py:338
  115.2 1.4 %copy.8 = f32[32,2,96]{2,1,0:T(2,128)} copy(f32[32,2,96]{2,0,1:T(8,128)} %bitcast.2) | data formatting | bytes 49152
  116.6 2.1 %copy.12 = bf16[384,1024]{1,0:T(8,128)(2,1)} copy(bf16[384,1024]{1,0:T(8,128)(2,1)} %get-tuple-element.20) | data formatting | bytes 1572864
  118.7 2.1 %copy.13 = bf16[384,1024]{1,0:T(8,128)(2,1)} copy(bf16[384,1024]{1,0:T(8,128)(2,1)} %get-tuple-element.21) | data formatting | bytes 1572864
  120.8 2.1 %copy.14 = bf16[384,1024]{1,0:T(8,128)(2,1)} copy(bf16[384,1024]{1,0:T(8,128)(2,1)} %get-tuple-element.22) | data formatting | bytes 1572864

commit v3 on v2

--- a/solution.py
+++ b/solution.py
@@ -54,21 +54,37 @@
         src = key_w if ch < nch else value_w
         return pltpu.make_async_copy(src.at[:, pl.ds((ch % nch) * CW, CW)], wb.at[ch], w_sem.at[ch])
 
-    load_w(0).start()
-    load_h(n_tp - 1).start()
-    load_h(0).start()
-    for ch in range(1, nch):
-        load_w(ch).start()
-    for b in range(1, n_tp - 1):
-        load_h(b).start()
-    for ch in range(nch, 2 * nch):
-        load_w(ch).start()
+    first = jnp.where(t < n_tp // 2, n_tp - 1, 0)
+    second = n_tp - 1 - first
+    piece, deep = rows // 3, wb.shape[1] // 2
+    for k in range(2):
+        part = pl.ds(k * deep, deep)
+        pltpu.make_async_copy(key_w.at[part, pl.ds(0, CW)], wb.at[0, part], w_sem.at[0]).start()
+    for k in range(3):
+        pltpu.make_async_copy(
+            hidden.at[pl.ds(first * rows + k * piece, piece), :], hb.at[first, pl.ds(k * piece, piece)], h_sem.at[first]
+        ).start()
 
     barrier = pltpu.get_barrier_semaphore()
     for d in range(1, n_tp):
         pl.semaphore_signal(barrier, inc=1, device_id={"tp": lax.rem(t + d, n_tp)}, device_id_type=MESH)
     for d in range(1, n_seq):
         pl.semaphore_signal(barrier, inc=1, device_id={"seq": lax.rem(s + d, n_seq)}, device_id_type=MESH)
+
+    load_w(0).wait()
+    load_h(first).wait()
+    for ch in range(1, nch):
+        load_w(ch).start()
+    load_h(second).start()
+    for b in range(1, n_tp - 1):
+        load_h(b).start()
+    for ch in range(nch, 2 * nch):
+        load_w(ch).start()
+
+    @pl.when((t == 0) | (t == n_tp - 1))
+    def _():
+        sb[first, 0] = jnp.dot(hb[first], wb[0], preferred_element_type=jnp.float32).astype(jnp.bfloat16)
+
     pl.semaphore_wait(barrier, n_tp - 1 + n_seq - 1)
 
     def send_right(b, ch):
@@ -249,35 +265,45 @@
         pltpu.make_async_copy(bnd_res, bounds_out, out_sem.at[2]).start()
 
     def forward_right(b, ch):
-        acc[...] = jnp.dot(hb[b], wb[ch], preferred_element_type=jnp.float32)
-
-        @pl.when(t > 0)
-        def _():
-            send_right(b, ch).wait_recv()
-            acc[...] += rr[b, ch].astype(jnp.float32)
-
-        sb[b, ch] = acc[...].astype(jnp.bfloat16)
+        @pl.when((t > 0) | (b < n_tp - 1) | (ch > 0))
+        def _():
+            acc[...] = jnp.dot(hb[b], wb[ch], preferred_element_type=jnp.float32)
+
+            @pl.when(t > 0)
+            def _():
+                send_right(b, ch).wait_recv()
+                acc[...] += rr[b, ch].astype(jnp.float32)
+
+            sb[b, ch] = acc[...].astype(jnp.bfloat16)
+
         send_right(b, ch).start()
 
     def forward_left(b, ch):
-        acc[...] = jnp.dot(hb[b], wb[ch], preferred_element_type=jnp.float32)
-
-        @pl.when(t < n_tp - 1)
-        def _():
-            send_left(b, ch).wait_recv()
-            acc[...] += rl[b, ch].astype(jnp.float32)
-
-        sb[b, ch] = acc[...].astype(jnp.bfloat16)
+        @pl.when((t < n_tp - 1) | (b > 0) | (ch > 0))
+        def _():
+            acc[...] = jnp.dot(hb[b], wb[ch], preferred_element_type=jnp.float32)
+
+            @pl.when(t < n_tp - 1)
+            def _():
+                send_left(b, ch).wait_recv()
+                acc[...] += rl[b, ch].astype(jnp.float32)
+
+            sb[b, ch] = acc[...].astype(jnp.bfloat16)
+
         send_left(b, ch).start()
 
     def body(i, carry):
         turn, c, ch = place(jnp.minimum(i, steps - 1))
 
-        @pl.when((turn == 0) & (i < steps))
+        @pl.when((turn == 0) & (i > 0) & (i < steps))
         def _():
             pltpu.make_async_copy(key_w.at[:, pl.ds(0, CW)], wb.at[ch], w_sem.at[ch]).wait()
 
-        for o in range(n_tp // 2):
+        @pl.when(i == 1)
+        def _():
+            load_h(second).wait()
+
+        for o in range(1, n_tp // 2):
             @pl.when(i == o * nch)
             def _(o=o):
                 load_h(o).wait()
@@ -321,6 +347,58 @@
     pltpu.make_async_copy(bnd_res, bounds_out, out_sem.at[2]).wait()
     for c in range(nch):
         pltpu.make_async_copy(values_s.at[c], values_out.at[:, pl.ds(c * CW, CW)], out_sem.at[3 + c]).wait()
+
+
+def write_kernel(keys, values, codes, bounds, keys_out, values_out, codes_out, bounds_out, rows_s, bnd_in, bnd_s, in_sem, out_sem):
+    parts = rows_s.shape[1]
+    size = rows_s.shape[2]
+    pairs = ((keys, keys_out), (values, values_out), (codes, codes_out))
+
+    def fetch_rows(k, p):
+        return pltpu.make_async_copy(pairs[k][0].at[pl.ds(p * size, size), :], rows_s.at[k, p], in_sem.at[k, p])
+
+    def store_rows(k, p):
+        return pltpu.make_async_copy(rows_s.at[k, p], pairs[k][1].at[pl.ds(p * size, size), :], out_sem.at[k, p])
+
+    fetch = pltpu.make_async_copy(bounds, bnd_in, in_sem.at[3, 0])
+    fetch.start()
+    every = [(k, p) for p in range(parts) for k in range(3)]
+    for k, p in every:
+        fetch_rows(k, p).start()
+    fetch.wait()
+    for side in range(2):
+        bnd_s[:, side, :] = bnd_in[side]
+    store = pltpu.make_async_copy(bnd_s, bounds_out, out_sem.at[3, 0])
+    store.start()
+    for k, p in every:
+        fetch_rows(k, p).wait()
+        store_rows(k, p).start()
+    for k, p in every:
+        store_rows(k, p).wait()
+    store.wait()
+
+
+def write_out(keys, values, codes, bounds):
+    rows, width = keys.shape
+    parts = 3
+    hbm = pl.BlockSpec(memory_space=pl.ANY)
+    bound_shape = (bounds.shape[1], 2, bounds.shape[2])
+    return pl.pallas_call(
+        write_kernel,
+        out_shape=[jax.ShapeDtypeStruct(a.shape, a.dtype) for a in (keys, values, codes)]
+        + [jax.ShapeDtypeStruct(bound_shape, bounds.dtype)],
+        in_specs=[hbm] * 4,
+        out_specs=[hbm] * 4,
+        scratch_shapes=[
+            pltpu.VMEM((3, parts, rows // parts, width), keys.dtype),
+            pltpu.VMEM(bounds.shape, bounds.dtype),
+            pltpu.VMEM(bound_shape, bounds.dtype),
+            pltpu.SemaphoreType.DMA((4, parts)),
+            pltpu.SemaphoreType.DMA((4, parts)),
+        ],
+        compiler_params=pltpu.CompilerParams(vmem_limit_bytes=60 * 2**20),
+        cost_estimate=pl.CostEstimate(flops=0, bytes_accessed=12 * rows * width, transcendentals=0),
+    )(keys, values, codes, bounds)
 
 
 def per_device(n_seq, n_tp, hidden_states, positions, key_weight, value_weight):
@@ -388,7 +466,7 @@
             transcendentals=0,
         ),
     )(hidden_states, positions.reshape(pages, PAGE), key_weight, value_weight)
-    return keys, values, codes, jnp.transpose(bounds, (1, 0, 2))
+    return write_out(keys, values, codes, bounds)
 
 
 def solution(mesh):

time: 123 us -> 117 us (0.951)
  local copies, waits for them, and re-layouts: 7.59 us -> 0 us
    unnamed x4 -> x0, local copies, waits for them, and re-layouts: 7.59 us -> none
    pallas_call x0 -> x1, Pallas kernels: none -> 2.57 us  [write_out(): pl.pallas_call(write_kernel, out_shape=[jax.ShapeDtypeStruct(a.shape, a.d...]
    pallas_call x1, Pallas kernels: 115 us -> 113 us  [per_device(): pl.pallas_call(functools.partial(kernel, n_seq, n_tp), out_shape=(jax.Sha...]
where the time goes in v3:
time: 117 us; the launch traced here: 116 us
  Pallas kernels  116 us (99%)
    pallas_call x1, Pallas kernels, per_device(): pl.pallas_call(functools.partial(kernel, n_seq, n_tp), out_shape=(jax.Sha...  113 us
    pallas_call x1, Pallas kernels, write_out(): pl.pallas_call(write_kernel, out_shape=[jax.ShapeDtypeStruct(a.shape, a.d...  2.57 us

profile of v3, /device:TPU:16, one launch (start us, length us, event | category | flops | bytes accessed | tf_op | source)
XLA Modules:
  0.0 116.5 jit_solution(4677590060033807490)
XLA Ops:
  0.6 113.3 %shard_map.75 = (bf16[384,1024]{1,0:T(8,128)(2,1)}, bf16[384,1024]{1,0:T(8,128)(2,1)}, bf16[384,1024]{1,0:T(8,128)(2,1)}, f32[2,32,96]{2,1,0:T(8,128)}) custom-call(bf16[1536,2048]{1,0:T(8,128)(2,1)} %hidden.1, s32[3,128]{1,0:T(4,128)} %bitcast.1, bf16[2048,1024]{1,0:T(8,128)(2,1)} %key_w.1, bf16[2048,1024]{1,0:T(8,128)(2,1)} %value_w.1), custom_call_target="tpu_custom_call" | custom-call | flops 12884901888 | bytes 17039360 | tf_op jit(solution)/shard_map/pallas_call | solution.py:416
  113.9 2.6 %shard_map.76 = (bf16[384,1024]{1,0:T(8,128)(2,1)}, bf16[384,1024]{1,0:T(8,128)(2,1)}, bf16[384,1024]{1,0:T(8,128)(2,1)}, f32[32,2,96]{2,1,0:T(2,128)}) custom-call(bf16[384,1024]{1,0:T(8,128)(2,1)} %get-tuple-element.8.keys, bf16[384,1024]{1,0:T(8,128)(2,1)} %get-tuple-element.9.values, bf16[384,1024]{1,0:T(8,128)(2,1)} %get-tuple-element.10.codes, ...), custom_call_target="tpu_custom_call" | custom-call | bytes 4718592 | tf_op jit(solution)/shard_map/pallas_call | solution.py:386

commit v4 on v3

--- a/solution.py
+++ b/solution.py
@@ -29,13 +29,12 @@
 
 def kernel(
     n_seq, n_tp,
-    hidden, pos, key_w, value_w,
+    hidden, pos_in, key_w, value_w,
     keys_out, values_out, codes_out, bounds_out,
-    hb, wb, sb, rr, rl, acc, raw, cos_s, sin_s,
-    keys_s, codes_s, values_s,
+    pos, hb, wb, sb, rr, rl, acc, raw, cos_s, sin_s,
     peak_own, peak_tp, peak_mid, peak_seq,
-    bnd_own, bnd_seq, bnd_tp, bnd_pages, bnd_turned, bnd_res,
-    h_sem, w_sem, send_sem, rr_sem, rl_sem, out_sem,
+    bnd_own, bnd_seq, bnd_tp, bnd_pages, bnd_turned,
+    pos_sem, h_sem, w_sem, send_sem, rr_sem, rl_sem,
     ptp_send, ptp_recv, psq_send, psq_recv, bsq_send, bsq_recv, btp_send, btp_recv,
 ):
     s = lax.axis_index("seq")
@@ -54,6 +53,12 @@
         src = key_w if ch < nch else value_w
         return pltpu.make_async_copy(src.at[:, pl.ds((ch % nch) * CW, CW)], wb.at[ch], w_sem.at[ch])
 
+    barrier = pltpu.get_barrier_semaphore()
+    for d in range(1, n_tp):
+        pl.semaphore_signal(barrier, inc=1, device_id={"tp": lax.rem(t + d, n_tp)}, device_id_type=MESH)
+    for d in range(1, n_seq):
+        pl.semaphore_signal(barrier, inc=1, device_id={"seq": lax.rem(s + d, n_seq)}, device_id_type=MESH)
+
     first = jnp.where(t < n_tp // 2, n_tp - 1, 0)
     second = n_tp - 1 - first
     piece, deep = rows // 3, wb.shape[1] // 2
@@ -65,17 +70,13 @@
             hidden.at[pl.ds(first * rows + k * piece, piece), :], hb.at[first, pl.ds(k * piece, piece)], h_sem.at[first]
         ).start()
 
-    barrier = pltpu.get_barrier_semaphore()
-    for d in range(1, n_tp):
-        pl.semaphore_signal(barrier, inc=1, device_id={"tp": lax.rem(t + d, n_tp)}, device_id_type=MESH)
-    for d in range(1, n_seq):
-        pl.semaphore_signal(barrier, inc=1, device_id={"seq": lax.rem(s + d, n_seq)}, device_id_type=MESH)
-
     load_w(0).wait()
     load_h(first).wait()
     for ch in range(1, nch):
         load_w(ch).start()
     load_h(second).start()
+    load_pos = pltpu.make_async_copy(pos_in, pos, pos_sem.at[0])
+    load_pos.start()
     for b in range(1, n_tp - 1):
         load_h(b).start()
     for ch in range(nch, 2 * nch):
@@ -123,6 +124,7 @@
         left_job(i - (n_tp - 1 - t), lambda b, ch: send_left(b, ch).wait_send())
 
     def fill_angles():
+        load_pos.wait()
         lane = lax.broadcasted_iota(jnp.int32, (1, HEAD), 1)
         half = HEAD // 2
         index = jnp.where(lane < half, lane, lane - half).astype(jnp.float32)
@@ -226,10 +228,10 @@
                 part = pl.ds(j * PAGE, PAGE)
                 ratio = raw[part, lanes] * inverse
                 code = (ratio - sine_of_turns(ratio) * (1.0 / (2.0 * math.pi))).astype(jnp.bfloat16)
-                codes_s[part, lanes] = code
+                codes_out[part, lanes] = code
                 dequant = code.astype(jnp.float32) * scale
                 turned = dequant * cos_s[part, :] + pltpu.roll(dequant, HEAD // 2, 1) * sin_s[part, :]
-                keys_s[part, lanes] = turned.astype(jnp.bfloat16)
+                keys_out[part, lanes] = turned.astype(jnp.bfloat16)
                 bnd_own[j:j + 1, lanes] = jnp.min(turned, axis=0, keepdims=True)
                 bnd_own[pages + j:pages + j + 1, lanes] = jnp.max(turned, axis=0, keepdims=True)
             return carry
@@ -237,8 +239,6 @@
         lax.fori_loop(0, width // HEAD, one, 0)
         for copy in bound_seq_copies():
             copy.start()
-        pltpu.make_async_copy(codes_s, codes_out, out_sem.at[0]).start()
-        pltpu.make_async_copy(keys_s, keys_out, out_sem.at[1]).start()
         bnd_seq[s] = bnd_own[:, tile_of(s)]
 
     def bounds_middle():
@@ -261,8 +261,7 @@
                     bnd_pages[first:first + pages, :] = bnd_tp[b, a, side * pages:(side + 1) * pages, :]
             bnd_turned[...] = jnp.transpose(bnd_pages[...])
             mine = bnd_turned[pl.ds(pl.multiple_of(inside, 8), channels), :]
-            bnd_res[side] = mine[:, :bnd_res.shape[2]]
-        pltpu.make_async_copy(bnd_res, bounds_out, out_sem.at[2]).start()
+            bounds_out[side] = mine[:, :bounds_out.shape[2]]
 
     def forward_right(b, ch):
         @pl.when((t > 0) | (b < n_tp - 1) | (ch > 0))
@@ -328,9 +327,7 @@
 
     def last(c, carry):
         own_sum(nch + c)
-        values_s[c] = acc[...].astype(jnp.bfloat16)
-        lanes = pl.ds(pl.multiple_of(c * CW, 128), CW)
-        pltpu.make_async_copy(values_s.at[c], values_out.at[:, lanes], out_sem.at[3 + c]).start()
+        values_out[:, pl.ds(pl.multiple_of(c * CW, 128), CW)] = acc[...].astype(jnp.bfloat16)
         return carry
 
     lax.fori_loop(0, nch, last, 0)
@@ -342,62 +339,36 @@
     lax.fori_loop(steps + n_tp - 2 - DEPTH, steps + n_tp - 2, drain, 0)
     for copy in peak_tp_copies() + peak_seq_copies() + bound_seq_copies() + bound_tp_copies():
         copy.wait_send()
-    pltpu.make_async_copy(codes_s, codes_out, out_sem.at[0]).wait()
-    pltpu.make_async_copy(keys_s, keys_out, out_sem.at[1]).wait()
-    pltpu.make_async_copy(bnd_res, bounds_out, out_sem.at[2]).wait()
-    for c in range(nch):
-        pltpu.make_async_copy(values_s.at[c], values_out.at[:, pl.ds(c * CW, CW)], out_sem.at[3 + c]).wait()
-
-
-def write_kernel(keys, values, codes, bounds, keys_out, values_out, codes_out, bounds_out, rows_s, bnd_in, bnd_s, in_sem, out_sem):
-    parts = rows_s.shape[1]
-    size = rows_s.shape[2]
-    pairs = ((keys, keys_out), (values, values_out), (codes, codes_out))
-
-    def fetch_rows(k, p):
-        return pltpu.make_async_copy(pairs[k][0].at[pl.ds(p * size, size), :], rows_s.at[k, p], in_sem.at[k, p])
-
-    def store_rows(k, p):
-        return pltpu.make_async_copy(rows_s.at[k, p], pairs[k][1].at[pl.ds(p * size, size), :], out_sem.at[k, p])
-
-    fetch = pltpu.make_async_copy(bounds, bnd_in, in_sem.at[3, 0])
-    fetch.start()
-    every = [(k, p) for p in range(parts) for k in range(3)]
-    for k, p in every:
-        fetch_rows(k, p).start()
-    fetch.wait()
+
+
+def write_kernel(keys, values, codes, bounds, keys_out, values_out, codes_out, bounds_out, bnd_s, sem):
+    half = keys.shape[0] // 2
+    moves = []
+    for k, (src, dst) in enumerate(((keys, keys_out), (values, values_out), (codes, codes_out))):
+        for p in range(2):
+            part = pl.ds(p * half, half)
+            moves.append(pltpu.make_async_copy(src.at[part, :], dst.at[part, :], sem.at[2 * k + p]))
+            moves[-1].start()
     for side in range(2):
-        bnd_s[:, side, :] = bnd_in[side]
-    store = pltpu.make_async_copy(bnd_s, bounds_out, out_sem.at[3, 0])
-    store.start()
-    for k, p in every:
-        fetch_rows(k, p).wait()
-        store_rows(k, p).start()
-    for k, p in every:
-        store_rows(k, p).wait()
-    store.wait()
+        bnd_s[:, side, :] = bounds[side]
+    moves.append(pltpu.make_async_copy(bnd_s, bounds_out, sem.at[6]))
+    moves[-1].start()
+    for move in moves:
+        move.wait()
 
 
 def write_out(keys, values, codes, bounds):
-    rows, width = keys.shape
-    parts = 3
     hbm = pl.BlockSpec(memory_space=pl.ANY)
     bound_shape = (bounds.shape[1], 2, bounds.shape[2])
     return pl.pallas_call(
         write_kernel,
         out_shape=[jax.ShapeDtypeStruct(a.shape, a.dtype) for a in (keys, values, codes)]
         + [jax.ShapeDtypeStruct(bound_shape, bounds.dtype)],
-        in_specs=[hbm] * 4,
+        in_specs=[pl.BlockSpec(memory_space=pltpu.VMEM)] * 4,
         out_specs=[hbm] * 4,
-        scratch_shapes=[
-            pltpu.VMEM((3, parts, rows // parts, width), keys.dtype),
-            pltpu.VMEM(bounds.shape, bounds.dtype),
-            pltpu.VMEM(bound_shape, bounds.dtype),
-            pltpu.SemaphoreType.DMA((4, parts)),
-            pltpu.SemaphoreType.DMA((4, parts)),
-        ],
-        compiler_params=pltpu.CompilerParams(vmem_limit_bytes=60 * 2**20),
-        cost_estimate=pl.CostEstimate(flops=0, bytes_accessed=12 * rows * width, transcendentals=0),
+        scratch_shapes=[pltpu.VMEM(bound_shape, bounds.dtype), pltpu.SemaphoreType.DMA((7,))],
+        compiler_params=pltpu.CompilerParams(vmem_limit_bytes=8 * 2**20),
+        cost_estimate=pl.CostEstimate(flops=0, bytes_accessed=12 * keys.size, transcendentals=0),
     )(keys, values, codes, bounds)
 
 
@@ -421,9 +392,10 @@
             jax.ShapeDtypeStruct((rows, width), bf16),
             jax.ShapeDtypeStruct((2, channels, all_pages), f32),
         ),
-        in_specs=[hbm, pl.BlockSpec(memory_space=pltpu.VMEM), hbm, hbm],
-        out_specs=(hbm, hbm, hbm, hbm),
+        in_specs=[pl.BlockSpec(memory_space=pltpu.HBM)] * 4,
+        out_specs=(pl.BlockSpec(memory_space=pltpu.VMEM),) * 4,
         scratch_shapes=[
+            pltpu.VMEM((pages, PAGE), jnp.int32),
             pltpu.VMEM((n_tp, rows, depth), bf16),
             pltpu.VMEM((2 * nch, depth, CW), bf16),
             pltpu.VMEM((n_tp, 2 * nch, rows, CW), bf16),
@@ -433,9 +405,6 @@
             pltpu.VMEM((rows, width), f32),
             pltpu.VMEM((rows, HEAD), f32),
             pltpu.VMEM((rows, HEAD), f32),
-            pltpu.VMEM((rows, width), bf16),
-            pltpu.VMEM((rows, width), bf16),
-            pltpu.VMEM((nch, rows, CW), bf16),
             pltpu.VMEM((8, width), f32),
             pltpu.VMEM((n_tp, 8, width), f32),
             pltpu.VMEM((8, width), f32),
@@ -445,20 +414,19 @@
             pltpu.VMEM((n_tp, n_seq, 8, tile), f32),
             pltpu.VMEM((padded_pages, tile), f32),
             pltpu.VMEM((tile, padded_pages), f32),
-            pltpu.VMEM((2, channels, all_pages), f32),
+            dma((1,)),
             dma((n_tp,)),
             dma((2 * nch,)),
             dma((n_tp, 2 * nch)),
             dma((n_tp, 2 * nch)),
             dma((n_tp, 2 * nch)),
-            dma((3 + nch,)),
             dma((n_tp,)), dma((n_tp,)),
             dma((n_seq,)), dma((n_seq,)),
             dma((n_seq,)), dma((n_seq,)),
             dma((n_tp,)), dma((n_tp,)),
         ],
         compiler_params=pltpu.CompilerParams(
-            collective_id=0, has_side_effects=True, vmem_limit_bytes=56 * 2**20
+            collective_id=0, has_side_effects=True, vmem_limit_bytes=48 * 2**20
         ),
         cost_estimate=pl.CostEstimate(
             flops=2 * n_tp * rows * depth * 2 * width,

time: 117 us -> 115 us (0.983)
  Pallas kernels: 116 us -> 114 us
where the time goes in v4:
time: 115 us
  Pallas kernels  114 us (99%)
    pallas_call x1, Pallas kernels, per_device(): pl.pallas_call(functools.partial(kernel, n_seq, n_tp), out_shape=(jax.Sha...  112 us

profile of v4, /device:TPU:16, one launch (start us, length us, event | category | flops | bytes accessed | tf_op | source)
XLA Modules:
  0.0 115.1 jit_solution(6769947482570625058)
XLA Ops:
  0.6 0.0 copy-start
  0.6 0.7 copy-done
  1.3 112.3 %shard_map.75 = (bf16[384,1024]{1,0:T(8,128)(2,1)S(1)}, bf16[384,1024]{1,0:T(8,128)(2,1)S(1)}, bf16[384,1024]{1,0:T(8,128)(2,1)S(1)}, f32[2,32,96]{2,1,0:T(8,128)S(1)}) custom-call(bf16[1536,2048]{1,0:T(8,128)(2,1)} %hidden.1, s32[3,128]{1,0:T(4,128)S(1)} %bitcast.1, bf16[2048,1024]{1,0:T(8,128)(2,1)} %key_w.1, bf16[2048,1024]{1,0:T(8,128)(2,1)} %value_w.1), custom_call_target="tpu_custom_call" | custom-call | flops 12884901888 | bytes 17039360 | tf_op jit(solution)/shard_map/pallas_call | solution.py:387
  113.7 1.5 %shard_map.76 = (bf16[384,1024]{1,0:T(8,128)(2,1)}, bf16[384,1024]{1,0:T(8,128)(2,1)}, bf16[384,1024]{1,0:T(8,128)(2,1)}, f32[32,2,96]{2,1,0:T(2,128)}) custom-call(bf16[384,1024]{1,0:T(8,128)(2,1)S(1)} %get-tuple-element.8.keys, bf16[384,1024]{1,0:T(8,128)(2,1)S(1)} %get-tuple-element.9.values, bf16[384,1024]{1,0:T(8,128)(2,1)S(1)} %get-tuple-element.10.codes, ...), custom_call_target="tpu_custom_call" | custom-call | bytes 4718592 | tf_op jit(solution)/shard_map/pallas_call | solution.py:363
Async XLA Ops:
  0.6 0.7 copy-start
